TPU v7x, 32 devices: a whole 2x2x4 slice. The times are simulated.
32 devices in a mesh: grp: 2 (over y), ctx: 1, mdl: 8 (over z, x), dp: 2 (over core).
Axes of the slice: x: 2, y: 2, z: 4, core: 2. Of those that a mesh axis runs over, the one named last changes fastest.
Arguments:
- layer_input: bfloat16 [4, 1024, 2560], P(('grp', 'dp'), 'ctx', 'mdl'), parts along dimension 0, may hold values from -6 to 6
- read_weight: bfloat16 [2560, 128], P('mdl'), may hold values from -0.125 to 0.125
- head_inputs: bfloat16 [4, 1024, 5120], P(('grp', 'dp'), 'ctx', 'mdl'), parts along dimension 0, may hold values from -6 to 6
- write_vectors: bfloat16 [4, 1024, 128], P(('grp', 'dp'), 'ctx'), parts along dimension 0, may hold values from -0.0034179688 to 0.0034179688
- log_decay: float32 [4, 80, 1024], P(('grp', 'dp'), 'mdl', 'ctx'), parts along dimension 0, may hold values from -1 to 0
- segment_ids: int32 [4, 1024], P(('grp', 'dp'), 'ctx'), parts along dimension 0, may hold values from 0 to 3, never falling along the last dimension, each value on 1 to 512 neighbouring positions
- out_grad: bfloat16 [4, 1024, 5120], P(('grp', 'dp'), 'ctx', 'mdl'), parts along dimension 0, may hold values from -0.0029296875 to 0.0029296875
Outputs:
- head_outputs: bfloat16 [4, 1024, 5120], P(('grp', 'dp'), 'ctx', 'mdl'), parts along dimension 0
- read_grad: float32 [256, 2560], P(('grp', 'ctx', 'dp'), 'mdl'), parts along dimension 0
There are 2 independent parts, one for each index of `grp`. A program takes and returns all parts, laid end to end along the dimension named above; an argument that names none is the same for every part. Nothing has to cross between parts.
Inputs may be any that keep to these rules, and one draw needn't show every extreme that they name: `segment_ids`: segment numbers never fall along a trace; each segment is a run of at most 512 positions.
All inputs are finite; a program needn't handle non-finite values.
Results may differ from a plain program's by a relative error of at most 0.015.
Values may be sent and summed in bfloat16 or wider, within the bound.
A program may use at most 64 MiB of HBM per device.

v0:
```python
import jax
import jax.numpy as jnp
from jax import lax
from jax.sharding import PartitionSpec as P

BLOCK_LEN = 512


def shifted(value, axis, by):
    count = lax.axis_size(axis)
    pairs = [(i, i + by) for i in range(count) if 0 <= i + by < count]
    return lax.ppermute(value, axis, pairs)


def join_parts(earlier, later):
    early_first, early_last, early_pass, leading_state = earlier
    later_first, later_last, later_pass, later_state = later
    linked = jnp.logical_or(
        early_last == later_first, jnp.logical_or(early_last < 0.0, later_first < 0.0)
    )
    carried = later_pass * linked.astype(jnp.float32)[..., None]
    front_seg = jnp.where(early_first < 0.0, later_first, early_first)
    back_seg = jnp.where(later_last < 0.0, early_last, later_last)
    return (
        front_seg,
        back_seg,
        early_pass * carried,
        later_state + carried[..., None, None] * leading_state,
    )


def per_device(
    layer_input, read_weight, head_inputs, write_vectors, log_decay, segment_ids, out_grad
):
    trace_count, length, model_cols = layer_input.shape
    head_count = log_decay.shape[1]
    head_dim = head_inputs.shape[2] // head_count
    state_dim = write_vectors.shape[2]
    block_count = length // BLOCK_LEN
    rows_all = trace_count * length
    flat_count = trace_count * block_count
    flat_input = layer_input.reshape(rows_all, model_cols)
    partial_value = jnp.dot(flat_input, read_weight, preferred_element_type=jnp.float32)
    readout = lax.psum(partial_value.astype(jnp.bfloat16), "mdl")
    segments = segment_ids.astype(jnp.float32).reshape(trace_count, block_count, BLOCK_LEN)
    decays = log_decay.reshape(trace_count, head_count, block_count, BLOCK_LEN)
    positions = jnp.arange(BLOCK_LEN)
    cumulative = jnp.cumsum(decays, axis=3)
    closing = cumulative[..., -1:]
    at_end = (segments == segments[..., -1:]).astype(jnp.float32)
    end_weight = jnp.exp(closing - cumulative) * at_end[:, None]
    values = head_inputs.reshape(trace_count, block_count, BLOCK_LEN, head_count, head_dim)
    keys_block = write_vectors.reshape(trace_count, block_count, BLOCK_LEN, state_dim)
    weighted = (values * jnp.transpose(end_weight, (0, 2, 3, 1))[..., None]).astype(jnp.bfloat16)
    block_states = jnp.einsum(
        "bkqhp,bkqn->kbhpn", weighted, keys_block, preferred_element_type=jnp.float32
    )
    front_seg = jnp.transpose(segments[..., 0])
    back_seg = jnp.transpose(segments[..., -1])
    single = (front_seg == back_seg).astype(jnp.float32)
    through = jnp.exp(jnp.transpose(closing[..., 0], (2, 0, 1))) * single[..., None]
    neutral = (
        -jnp.ones((trace_count,), jnp.float32),
        -jnp.ones((trace_count,), jnp.float32),
        jnp.ones((trace_count, head_count), jnp.float32),
        jnp.zeros((trace_count, head_count, head_dim, state_dim), jnp.float32),
    )

    def absorb(running, pieces):
        return (join_parts(running, pieces), running)

    device_total, prefixes = lax.scan(absorb, neutral, (front_seg, back_seg, through, block_states))
    position = lax.axis_index("ctx")

    def relay_once(iteration, incoming):
        outgoing = join_parts(incoming, device_total)
        shifted_lines = shifted((outgoing[0], outgoing[1], outgoing[2], outgoing[3]), "ctx", 1)
        return tuple(
            (
                jnp.where(position == 0, anchor, arrived)
                for anchor, arrived in zip(neutral, shifted_lines)
            )
        )

    entering = lax.fori_loop(0, lax.axis_size("ctx") - 1, relay_once, neutral)
    starts = join_parts(entering, prefixes)
    start_low = starts[3].astype(jnp.bfloat16)
    prior_seg = jnp.transpose(starts[1])
    coupled_items = (segments == prior_seg[..., None]).astype(jnp.float32)
    entry_gain = jnp.exp(cumulative) * coupled_items[:, None]
    gain_rows = jnp.transpose(entry_gain, (0, 2, 3, 1))[..., None]
    readout_block = readout.reshape(trace_count, block_count, BLOCK_LEN, state_dim)
    grads_block = out_grad.reshape(trace_count, block_count, BLOCK_LEN, head_count, head_dim)
    carried_out = (
        jnp.einsum(
            "bkqn,kbhpn->bkqhp", readout_block, start_low, preferred_element_type=jnp.float32
        )
        * gain_rows
    )
    per_head = jnp.einsum(
        "bkqhp,kbhpn->bkqhn", grads_block, start_low, preferred_element_type=jnp.float32
    )
    carried_back = jnp.sum(per_head * gain_rows, axis=3)
    causal = positions[:, None] >= positions[None, :]

    def inside(pieces):
        read_rows, key_rows, value_rows, grad_rows, cum_rows, seg_rows = pieces
        allowed = jnp.logical_and(causal, seg_rows[:, None] == seg_rows[None, :])
        spread = cum_rows[:, :, None] - cum_rows[:, None, :]
        weight = jnp.where(allowed[None], jnp.exp(jnp.where(allowed[None], spread, 0.0)), 0.0)
        scores = jnp.einsum("tn,sn->ts", read_rows, key_rows, preferred_element_type=jnp.float32)
        blend_factor = (weight * scores[None]).astype(jnp.bfloat16)
        inside_out = jnp.einsum(
            "hts,shp->thp", blend_factor, value_rows, preferred_element_type=jnp.float32
        )
        products = jnp.einsum(
            "thp,shp->hts", grad_rows, value_rows, preferred_element_type=jnp.float32
        )
        response = jnp.sum(weight * products, axis=0).astype(jnp.bfloat16)
        inside_back = jnp.dot(response, key_rows, preferred_element_type=jnp.float32)
        return (inside_out, inside_back)

    own_out, own_back = lax.map(
        inside,
        (
            readout_block.reshape(flat_count, BLOCK_LEN, state_dim),
            keys_block.reshape(flat_count, BLOCK_LEN, state_dim),
            values.reshape(flat_count, BLOCK_LEN, head_count, head_dim),
            grads_block.reshape(flat_count, BLOCK_LEN, head_count, head_dim),
            jnp.transpose(cumulative, (0, 2, 1, 3)).reshape(flat_count, head_count, BLOCK_LEN),
            segments.reshape(flat_count, BLOCK_LEN),
        ),
    )
    total_out = (
        own_out.reshape(trace_count, block_count, BLOCK_LEN, head_count, head_dim) + carried_out
    )
    head_outputs = total_out.astype(jnp.bfloat16).reshape(
        trace_count, length, head_count * head_dim
    )
    back_part = (
        own_back.reshape(trace_count, block_count, BLOCK_LEN, state_dim) + carried_back
    ).reshape(rows_all, state_dim)
    read_back = lax.psum(back_part.astype(jnp.bfloat16), "mdl")
    read_grad = lax.psum_scatter(
        lax.dot_general(
            read_back, flat_input, (((0,), (0,)), ((), ())), preferred_element_type=jnp.float32
        ),
        ("ctx", "dp"),
        scatter_dimension=0,
        tiled=True,
    )
    return (head_outputs, read_grad)


def solution(mesh):
    placed = (
        P(("grp", "dp"), "ctx", "mdl"),
        P("mdl", None),
        P(("grp", "dp"), "ctx", "mdl"),
        P(("grp", "dp"), "ctx", None),
        P(("grp", "dp"), "mdl", "ctx"),
        P(("grp", "dp"), "ctx"),
        P(("grp", "dp"), "ctx", "mdl"),
    )
    return jax.shard_map(
        per_device,
        mesh=mesh,
        in_specs=placed,
        out_specs=(P(("grp", "dp"), "ctx", "mdl"), P(("grp", "ctx", "dp"), "mdl")),
        check_vma=False,
    )
```

profile of v0, /device:TPU:0, one launch (start us, length us, event | category | flops | bytes accessed | tf_op | source)
XLA Modules:
  0.0 198.6 jit_solution(15188353820331368359)
XLA Ops:
  8.3 2.0 %convolution_convert_fusion = bf16[1024,128]{1,0:T(8,128)(2,1)} fusion(bf16[320,128]{1,0:T(8,128)(2,1)} %param.12, bf16[1,1024,320]{1,2,0:T(8,128)(2,1)S(1)} %copy-done), kind=kOutput, calls=%fused_computation.50 | convolution fusion | flops 84017152 | bytes 999424 | tf_op jit(solution)/shard_map/dot_general | solution.py:43
  11.1 2.3 %reduce-window.6 = f32[1,10,2,4,128]{4,1,2,3,0:T(8,128)S(1)} reduce-window(f32[1,10,2,4,128]{4,1,2,3,0:T(8,128)S(1)} %copy.90, f32[]{:T(128)} %constant.61.clone.1), window={size=1x1x1x1x128 pad=0_0x0_0x0_0x0_0x127_0}, to_apply=%region_1.0 | reduce-window | flops 1300480 | bytes 81924 | tf_op jit(solution)/shard_map/reduce-window
  17.0 2.4 %copy.89 = bf16[1,1024,640]{1,2,0:T(8,128)(2,1)} copy(bf16[1,1024,640]{2,1,0:T(8,128)(2,1)} %param.13) | data formatting | bytes 2621440 | tf_op args[2]
  19.4 3.6 %reshape_reshape.15 = bf16[2,512,10,64]{1,0,3,2:T(2,128)(2,1)S(1)} reshape(bf16[1,1024,640]{1,2,0:T(8,128)(2,1)} %copy.89) | data formatting | bytes 2621440 | tf_op jit(solution)/shard_map/reshape;reshape | solution.py:128
  24.3 2.3 %multiply_convert_fusion.6 = bf16[2,512,10,64]{1,0,3,2:T(2,128)(2,1)} fusion(bf16[2,512,10,64]{1,0,3,2:T(2,128)(2,1)S(1)} %reshape_reshape.15, f32[2,512,10]{1,0,2:T(2,128)S(1)} %copy.103), kind=kLoop, calls=%fused_computation.46 | loop fusion | flops 1966080 | bytes 2662400 | tf_op jit(solution)/shard_map/convert_element_type | solution.py:54
  26.7 1.8 fusion.32
  28.6 8.4 %while.40 = (s32[]{:T(128)}, f32[1]{0:T(128)}, f32[1,10]{1,0:T(1,128)S(1)}, f32[1,10,64,128]{3,2,1,0:T(8,128)S(1)}, f32[2,1]{0,1:T(1,128)S(1)}, /*index=5*/f32[2...) while((s32[]{:T(128)}, f32[1]{0:T(128)}, ...), condition=%wide.region_7.8_spmd.clone.clone, body=%wide.region_6.7_spmd.clone.sunk.clone | while | flops 327741 | bytes 1640430 | solution.py:72
  38.1 2.5 %copy.96 = bf16[1,1024,640]{1,2,0:T(8,128)(2,1)} copy(bf16[1,1024,640]{2,1,0:T(8,128)(2,1)} %param.17) | data formatting | bytes 2621440 | tf_op args[6]
  40.6 3.6 %reshape_reshape.19 = bf16[2,512,10,64]{1,0,3,2:T(2,128)(2,1)S(1)} reshape(bf16[1,1024,640]{1,2,0:T(8,128)(2,1)} %copy.96) | data formatting | bytes 2621440 | tf_op jit(solution)/shard_map/reshape;reshape | solution.py:129
  44.4 1.4 copy.99
  45.7 3.0 %fusion.29 = f32[2,512,128]{1,2,0:T(8,128)} fusion(f32[2,512,10]{1,2,0:T(8,128)S(1)} %copy.108, f32[2,1,10,64,128]{4,3,2,1,0:T(8,128)} %get-tuple-element.146, f32[2,10]{1,0:T(2,128)S(1)} %bitcast.194, bf16[2,512,10,64]{1,0,3,2:T(2,128)(2,1)S(1)} %reshape_reshape.19), kind=kOutput, calls=%fused_computation.44 | convolution fusion | flops 170590208 | bytes 2531408 | tf_op jit(solution)/shard_map/bkqhp,kbhpn->bkqhn/dot_general | solution.py:100
  48.7 35.9 %all-reduce.3.cloned.1.call-done = bf16[2,512,128]{2,1,0:T(8,128)(2,1)} async-done(((bf16[2,512,128]{2,1,0:T(8,128)(2,1)}), bf16[2,512,128]{2,1,0:T(8,128)(2,1)}) %all-reduce.3.cloned.1.call-update) | async-done | bytes 262160 | tf_op jit(solution)/shard_map/psum | solution.py:44
  84.7 23.7 %while.39 = (s32[]{:T(128)}, f32[2,512,10,64]{1,3,2,0:T(8,128)}, f32[2,512,128]{1,2,0:T(8,128)}, bf16[2,512,10,64]{1,3,2,0:T(8,128)(2,1)}, f32[2,512]{1,0:T(2,12...) while((s32[]{:T(128)}, f32[2,512,10,64]{1,3,2,0:T(8,128)}, ...), condition=%wide.region_5.6_spmd.clone.clone, body=%wide.region_3.5_spmd.clone.sunk.clone | while | flops 832045056 | bytes 18532508 | solution.py:123
  86.1 5.5 %fusion.82 = f32[2,512,10,64]{1,3,2,0:T(8,128)} fusion(f32[2,512,10,64]{1,3,2,0:T(8,128)} %get-tuple-element.535, s32[]{:T(128)} %get-tuple-element.534, f32[512,512]{1,0:T(8,128)S(1)} %fusion.80, f32[10,512]{1,0:T(8,128)S(1)} %dynamic-slice_bitcast_fusion.3, pred[512,512]{1,0:T(8,128)(4,1)S(1)} %fusion.81, ...), kind=kOutput, calls=%fused_computation.7.clone.1.clone | convolution fusion | flops 348651520 | bytes 3343360 | tf_op jit(solution)/shard_map/while/body/eval_jaxpr/hts,shp->thp/dot_general | solution.py:113
  91.7 3.8 %multiply_reduce_fusion.3 = bf16[512,512]{1,0:T(8,128)(2,1)S(1)} fusion(f32[10,512]{1,0:T(8,128)S(1)} %dynamic-slice_bitcast_fusion.3, pred[512,512]{1,0:T(8,128)(4,1)S(1)} %fusion.81, bf16[2,512,10,64]{1,3,2,0:T(8,128)(2,1)S(1)} %copy-done.5, s32[]{:T(128)} %get-tuple-element.534, bf16[2,512,10,64]{1,3,2,0:T(8,128)(2,1)S(1)} %copy-done.4), kind=kOutput, calls=%fused_computation.1.clone.1.clone | convolution fusion | flops 348389376 | bytes 2163712 | tf_op jit(solution)/shard_map/while/body/eval_jaxpr/thp,shp->hts/dot_general | solution.py:116
  98.0 5.5 %fusion.82 = f32[2,512,10,64]{1,3,2,0:T(8,128)} fusion(f32[2,512,10,64]{1,3,2,0:T(8,128)} %get-tuple-element.535, s32[]{:T(128)} %get-tuple-element.534, f32[512,512]{1,0:T(8,128)S(1)} %fusion.80, f32[10,512]{1,0:T(8,128)S(1)} %dynamic-slice_bitcast_fusion.3, pred[512,512]{1,0:T(8,128)(4,1)S(1)} %fusion.81, ...), kind=kOutput, calls=%fused_computation.7.clone.1.clone | convolution fusion | flops 348651520 | bytes 3343360 | tf_op jit(solution)/shard_map/while/body/eval_jaxpr/hts,shp->thp/dot_general | solution.py:113
  103.5 3.8 %multiply_reduce_fusion.3 = bf16[512,512]{1,0:T(8,128)(2,1)S(1)} fusion(f32[10,512]{1,0:T(8,128)S(1)} %dynamic-slice_bitcast_fusion.3, pred[512,512]{1,0:T(8,128)(4,1)S(1)} %fusion.81, bf16[2,512,10,64]{1,3,2,0:T(8,128)(2,1)S(1)} %copy-done.5, s32[]{:T(128)} %get-tuple-element.534, bf16[2,512,10,64]{1,3,2,0:T(8,128)(2,1)S(1)} %copy-done.4), kind=kOutput, calls=%fused_computation.1.clone.1.clone | convolution fusion | flops 348389376 | bytes 2163712 | tf_op jit(solution)/shard_map/while/body/eval_jaxpr/thp,shp->hts/dot_general | solution.py:116
  108.4 2.1 %add_convert_fusion.2 = bf16[2,512,128]{1,2,0:T(8,128)(2,1)} fusion(f32[2,512,128]{1,2,0:T(8,128)} %get-tuple-element.149, f32[2,512,128]{1,2,0:T(8,128)} %fusion.29), kind=kLoop, calls=%fused_computation.56 | loop fusion | flops 262144 | bytes 1310720 | tf_op jit(solution)/shard_map/convert_element_type | solution.py:143
  110.5 1.8 copy.113
  112.4 70.0 %all-reduce.5.cloned.1.call-done = bf16[1024,128]{1,0:T(8,128)(2,1)} async-done(((bf16[1024,128]{1,0:T(8,128)(2,1)}), bf16[1024,128]{1,0:T(8,128)(2,1)}) %all-reduce.5.cloned.1.call-update) | async-done | bytes 262160 | tf_op jit(solution)/shard_map/psum | solution.py:143
  182.4 2.0 %fusion.35 = f32[128,320]{1,0:T(8,128)} fusion(bf16[1024,128]{1,0:T(8,128)(2,1)} %all-reduce.5.cloned.1.call-done, bf16[1,1024,320]{1,2,0:T(8,128)(2,1)S(1)} %copy-done), kind=kOutput, calls=%fused_computation.51 | convolution fusion | flops 83886080 | bytes 1081344 | tf_op jit(solution)/shard_map/dot_general | solution.py:145
  184.4 1.6 add_convert_fusion
  188.4 1.4 copy.114
  189.8 2.3 %reduce-scatter.2.cloned.1.call-done = f32[64,320]{1,0:T(8,128)} async-done(((f32[128,320]{1,0:T(8,128)}), f32[64,320]{1,0:T(8,128)}) %reduce-scatter.2.cloned.1.call-update) | async-done | bytes 81936 | tf_op jit(solution)/shard_map/reduce_scatter | solution.py:144
  (88 shorter events, 18.7 us)
Async XLA Ops:
  7.2 1.1 copy-start
  7.2 77.5 %all-reduce.3.cloned.1.call-start = ((), (), s32[]{:S(2)}) async-start(), calls=%async_computation.1 | async-start | bytes 524288 | tf_op jit(solution)/shard_map/psum | solution.py:44
  10.3 172.1 %all-reduce.5.cloned.1.call-start = ((), (), s32[]{:S(2)}) async-start(), calls=%async_computation.2 | async-start | bytes 524288 | tf_op jit(solution)/shard_map/psum | solution.py:143
  23.0 3.8 %copy-start.1 = (bf16[1,1024,128]{2,1,0:T(8,128)(2,1)S(1)}, bf16[1,1024,128]{2,1,0:T(8,128)(2,1)}, u32[]{:S(2)}) copy-start(bf16[1,1024,128]{2,1,0:T(8,128)(2,1)} %param.14) | copy-start | bytes 786436
  38.1 7.6 %copy-start.6 = (f32[2,512,10]{1,2,0:T(8,128)}, f32[2,512,10]{1,2,0:T(8,128)S(1)}, u32[]{:S(2)}) copy-start(f32[2,512,10]{1,2,0:T(8,128)S(1)} %copy.108) | copy-start | bytes 122884
  86.1 5.5 %copy-start.4 = (bf16[2,512,10,64]{1,3,2,0:T(8,128)(2,1)S(1)}, bf16[2,512,10,64]{1,3,2,0:T(8,128)(2,1)}, u32[]{:S(2)}) copy-start(bf16[2,512,10,64]{1,3,2,0:T(8,128)(2,1)} %get-tuple-element.546) | copy-start | bytes 3932164 | tf_op jit(solution)/shard_map/while
  86.1 5.5 %copy-start.5 = (bf16[2,512,10,64]{1,3,2,0:T(8,128)(2,1)S(1)}, bf16[2,512,10,64]{1,3,2,0:T(8,128)(2,1)}, u32[]{:S(2)}) copy-start(bf16[2,512,10,64]{1,3,2,0:T(8,128)(2,1)} %get-tuple-element.551) | copy-start | bytes 3932164 | tf_op jit(solution)/shard_map/while
  98.0 5.6 %copy-start.4 = (bf16[2,512,10,64]{1,3,2,0:T(8,128)(2,1)S(1)}, bf16[2,512,10,64]{1,3,2,0:T(8,128)(2,1)}, u32[]{:S(2)}) copy-start(bf16[2,512,10,64]{1,3,2,0:T(8,128)(2,1)} %get-tuple-element.546) | copy-start | bytes 3932164 | tf_op jit(solution)/shard_map/while
  98.0 5.5 %copy-start.5 = (bf16[2,512,10,64]{1,3,2,0:T(8,128)(2,1)S(1)}, bf16[2,512,10,64]{1,3,2,0:T(8,128)(2,1)}, u32[]{:S(2)}) copy-start(bf16[2,512,10,64]{1,3,2,0:T(8,128)(2,1)} %get-tuple-element.551) | copy-start | bytes 3932164 | tf_op jit(solution)/shard_map/while
  108.4 76.0 %copy-start.2 = (bf16[2,512,128]{2,1,0:T(8,128)(2,1)S(1)}, bf16[2,512,128]{2,1,0:T(8,128)(2,1)}, u32[]{:S(2)}) copy-start(bf16[2,512,128]{2,1,0:T(8,128)(2,1)} %get-tuple-element.592) | copy-start | bytes 786436
  108.4 76.0 %copy-start.3 = (f32[2,512,10,64]{1,3,2,0:T(8,128)S(1)}, f32[2,512,10,64]{1,3,2,0:T(8,128)}, u32[]{:S(2)}) copy-start(f32[2,512,10,64]{1,3,2,0:T(8,128)} %get-tuple-element.145) | copy-start | bytes 7864324
  112.4 79.7 %reduce-scatter.2.cloned.1.call-start = ((), (), s32[]{:S(2)}) async-start(), calls=%async_computation.3 | async-start | bytes 294912 | tf_op jit(solution)/shard_map/reduce_scatter | solution.py:144
Sparse Core Ops, SparseCore 0:
  11.4 73.2 all-reduce.2
  112.5 69.8 all-reduce.4
  185.2 6.8 reduce-scatter.1
where the time goes:
time: 199 us
  waiting for transfers between devices  108 us (54%)
  matrix products  33.6 us (17%)
  local copies, waits for them, and re-layouts  25.3 us (13%)
  between operations  14 us (7%)
  other arithmetic  12.1 us (6%)
  loops' own time  5.3 us (3%)
    psum x1, waiting for transfers between devices, per_device(): read_back = lax.psum(back_part.astype(jnp.bfloat16), 'mdl')  70 us
    psum x1, waiting for transfers between devices, per_device(): readout = lax.psum(partial_value.astype(jnp.bfloat16), 'mdl')  35.9 us
    dot_general x2, matrix products, inside(): jnp.einsum('hts,shp->thp', blend_factor, value_rows, preferred_element_ty...  11.1 us
    unnamed x19, local copies, waits for them, and re-layouts  10.5 us
    dot_general x2, matrix products, inside(): jnp.einsum('thp,shp->hts', grad_rows, value_rows, preferred_element_type=...  7.62 us
    another operation x1, loops' own time, per_device(): lax.scan(absorb, neutral, (front_seg, back_seg, through, block_states))  5.19 us
  transfers between devices with their start and end apart: 3, of which 3 were waited for; matrix products, arithmetic and copies ran while one was open for 19% of the time, Pallas kernels for 0%

commit v1 on v0

--- a/solution.py
+++ b/solution.py
@@ -1,9 +1,19 @@
 import jax
 import jax.numpy as jnp
 from jax import lax
+from jax.experimental import pallas as pl
+from jax.experimental.pallas import tpu as pltpu
 from jax.sharding import PartitionSpec as P
 
 BLOCK_LEN = 512
+MESH = pl.DeviceIdType.MESH
+MDL = 8
+SHARE = 2 * BLOCK_LEN // MDL
+HALF = BLOCK_LEN // MDL
+HEAD_N = 10
+PAIRS = HEAD_N // 2
+TILE = 256
+LOG2E = 1.4426950408889634
 
 
 def shifted(value, axis, by):
@@ -45,7 +55,8 @@
     segments = segment_ids.astype(jnp.float32).reshape(trace_count, block_count, BLOCK_LEN)
     decays = log_decay.reshape(trace_count, head_count, block_count, BLOCK_LEN)
     positions = jnp.arange(BLOCK_LEN)
-    cumulative = jnp.cumsum(decays, axis=3)
+    upper = (positions[:, None] <= positions[None, :]).astype(jnp.float32)
+    cumulative = jnp.einsum("bhks,st->bhkt", decays, upper, precision=lax.Precision.HIGHEST)
     closing = cumulative[..., -1:]
     at_end = (segments == segments[..., -1:]).astype(jnp.float32)
     end_weight = jnp.exp(closing - cumulative) * at_end[:, None]
@@ -152,7 +163,274 @@
     return (head_outputs, read_grad)
 
 
+def fused_kernel(
+    x_ref, w_ref, hi_ref, wv_ref, ld_ref, seg_ref, og_ref, out_ref, grad_ref,
+    part, rs1, readout, back, rs2, rb, gfull, grecv,
+    split, stack, rowx, colx, endx, entx, bias, resp, scores, start, carry,
+    rs1_s, rs1_r, ag1_s, ag1_r, rs2_s, rs2_r, ag2_s, ag2_r, dp_s, dp_r,
+):
+    f32, bf16 = jnp.float32, jnp.bfloat16
+    me = lax.axis_index("mdl")
+    core = lax.axis_index("dp")
+    peers = [lax.rem(me + o, MDL) for o in range(MDL)]
+    barrier = pltpu.get_barrier_semaphore()
+    for o in range(1, MDL):
+        pl.semaphore_signal(barrier, inc=1, device_id={"mdl": peers[o]}, device_id_type=MESH)
+    pl.semaphore_signal(barrier, inc=1, device_id={"dp": 1 - core}, device_id_type=MESH)
+
+    def remote(src, dst, send, recv, to):
+        copy = pltpu.make_async_remote_copy(
+            src_ref=src, dst_ref=dst, send_sem=send, recv_sem=recv,
+            device_id=to, device_id_type=MESH,
+        )
+        copy.start()
+        return copy
+
+    part[...] = jnp.dot(x_ref[...], w_ref[...], preferred_element_type=f32).astype(bf16)
+    pl.semaphore_wait(barrier, MDL)
+    first = [
+        remote(
+            part.at[pl.ds(pl.multiple_of(peers[o] * SHARE, SHARE), SHARE)], rs1.at[o],
+            rs1_s.at[o], rs1_r.at[o], {"mdl": peers[o]},
+        )
+        for o in range(1, MDL)
+    ]
+
+    lane = lax.broadcasted_iota(jnp.int32, (1, 128), 1)
+    left = lane < 64
+    mask_a = left.astype(f32).astype(bf16)
+    mask_b = (1.0 - left.astype(f32)).astype(bf16)
+    rows_i = lax.broadcasted_iota(jnp.int32, (BLOCK_LEN, BLOCK_LEN), 0)
+    cols_i = lax.broadcasted_iota(jnp.int32, (BLOCK_LEN, BLOCK_LEN), 1)
+    upper = (rows_i <= cols_i).astype(f32).astype(bf16)
+    nn = (((1,), (1,)), ((), ()))
+    tt = (((0,), (0,)), ((), ()))
+
+    def prepare(k):
+        span = pl.ds(k * BLOCK_LEN, BLOCK_LEN)
+        split[...] = jnp.zeros_like(split)
+        stack[...] = jnp.zeros_like(stack)
+        rest = ld_ref[0, :, span]
+        for piece in range(3):
+            high = rest.astype(bf16).astype(f32)
+            split[pl.ds(16 * piece, HEAD_N), :] = high
+            rest = rest - high
+        sums = jnp.dot(split[...].astype(bf16), upper, preferred_element_type=f32)
+        cum = (sums[0:16] + sums[16:32] + sums[32:48]) * LOG2E
+        seg = seg_ref[:, span].astype(f32)
+        stack[pl.ds(0, 16), :] = cum
+        if k == 0:
+            close = cum[:, BLOCK_LEN - 1 :]
+            at_end = (seg == seg[:, BLOCK_LEN - 1 :]).astype(f32)
+            stack[pl.ds(16, 16), :] = jnp.exp2(close - cum) * at_end
+        else:
+            prior = seg_ref[:, pl.ds(BLOCK_LEN - 128, 128)].astype(f32)[:, 127:]
+            stack[pl.ds(32, 16), :] = jnp.exp2(cum) * (seg == prior).astype(f32)
+        stack[pl.ds(48, 8), :] = jnp.broadcast_to(seg, (8, BLOCK_LEN))
+        turned = stack[...].T
+        for h in range(HEAD_N):
+            rowx[k, h] = cum[h : h + 1, :]
+            colx[k, h] = jnp.broadcast_to(turned[:, h : h + 1], (BLOCK_LEN, 128))
+        for j in range(PAIRS):
+            base, target = (16, endx) if k == 0 else (32, entx)
+            a = turned[:, base + 2 * j : base + 2 * j + 1]
+            b = turned[:, base + 2 * j + 1 : base + 2 * j + 2]
+            target[j] = jnp.where(left, a, b)
+        same = jnp.logical_and(turned[:, 48:49] == seg, rows_i >= cols_i)
+        bias[k] = jnp.where(same, 0.0, -1e30)
+
+    def weight(k, h, i, wide):
+        rows = pl.ds(i * TILE, TILE)
+        col = colx[k, h, rows, :]
+        col = jnp.concatenate([col] * (wide // 128), axis=1)
+        return jnp.exp2((col - rowx[k, h, :, pl.ds(0, wide)]) + bias[k, rows, pl.ds(0, wide)])
+
+    def lanes_of(j):
+        return pl.ds(pl.multiple_of(j * 128, 128), 128)
+
+    def backward(k):
+        resp[...] = jnp.zeros_like(resp)
+        carry[...] = jnp.zeros_like(carry)
+        keys = wv_ref[0, pl.ds(k * BLOCK_LEN, BLOCK_LEN), :]
+
+        def body(j, _):
+            lanes = lanes_of(j)
+            if k == 0:
+                value = hi_ref[0, pl.ds(0, BLOCK_LEN), lanes].astype(f32)
+                low = (value * endx[j]).astype(bf16)
+                start[j] = lax.dot_general(low, keys, tt, preferred_element_type=f32).astype(bf16)
+            else:
+                grads = og_ref[0, pl.ds(BLOCK_LEN, BLOCK_LEN), lanes].astype(f32)
+                carry[...] += jnp.dot(
+                    (grads * entx[j]).astype(bf16), start[j], preferred_element_type=f32
+                )
+            for i in range(BLOCK_LEN // TILE):
+                wide = (i + 1) * TILE
+                value = hi_ref[0, pl.ds(k * BLOCK_LEN, wide), lanes]
+                grads = og_ref[0, pl.ds(k * BLOCK_LEN + i * TILE, TILE), lanes]
+                pa = lax.dot_general(grads * mask_a, value, nn, preferred_element_type=f32)
+                pb = lax.dot_general(grads * mask_b, value, nn, preferred_element_type=f32)
+                resp[pl.ds(i * TILE, TILE), pl.ds(0, wide)] += (
+                    weight(k, 2 * j, i, wide) * pa + weight(k, 2 * j + 1, i, wide) * pb
+                )
+            return 0
+
+        lax.fori_loop(0, PAIRS, body, 0)
+        total = jnp.dot(resp[...].astype(bf16), keys, preferred_element_type=f32) + carry[...]
+        back[pl.ds(k * BLOCK_LEN, BLOCK_LEN), :] = total.astype(bf16)
+        return [
+            remote(
+                back.at[pl.ds(pl.multiple_of(k * BLOCK_LEN + peers[o] * HALF, HALF), HALF)],
+                rs2.at[k, o], rs2_s.at[k, o], rs2_r.at[k, o], {"mdl": peers[o]},
+            )
+            for o in range(1, MDL)
+        ]
+
+    def forward(k):
+        keys = wv_ref[0, pl.ds(k * BLOCK_LEN, BLOCK_LEN), :]
+        reads = readout[pl.ds(k * BLOCK_LEN, BLOCK_LEN), :]
+        scores[...] = lax.dot_general(reads, keys, nn, preferred_element_type=f32)
+
+        def body(j, _):
+            lanes = lanes_of(j)
+            for i in range(BLOCK_LEN // TILE):
+                wide = (i + 1) * TILE
+                value = hi_ref[0, pl.ds(k * BLOCK_LEN, wide), lanes]
+                score = scores[pl.ds(i * TILE, TILE), pl.ds(0, wide)]
+                oa = jnp.dot(
+                    (weight(k, 2 * j, i, wide) * score).astype(bf16), value,
+                    preferred_element_type=f32,
+                )
+                ob = jnp.dot(
+                    (weight(k, 2 * j + 1, i, wide) * score).astype(bf16), value,
+                    preferred_element_type=f32,
+                )
+                total = jnp.where(left, oa, ob)
+                if k == 1:
+                    carried = lax.dot_general(
+                        readout[pl.ds(BLOCK_LEN + i * TILE, TILE), :], start[j], nn,
+                        preferred_element_type=f32,
+                    )
+                    total = total + carried * entx[j, pl.ds(i * TILE, TILE), :]
+                out_ref[0, pl.ds(k * BLOCK_LEN + i * TILE, TILE), lanes] = total.astype(bf16)
+            return 0
+
+        lax.fori_loop(0, PAIRS, body, 0)
+
+    def collect(k, copies):
+        mine = pl.ds(pl.multiple_of(k * BLOCK_LEN + me * HALF, HALF), HALF)
+        total = back[mine, :].astype(f32)
+        for o in range(1, MDL):
+            copies[o - 1].wait_recv()
+            total = total + rs2[k, o].astype(f32)
+        rb[mine, :] = total.astype(bf16)
+        return [
+            remote(rb.at[mine], rb.at[mine], ag2_s.at[k, o], ag2_r.at[k, o], {"mdl": peers[o]})
+            for o in range(1, MDL)
+        ]
+
+    prepare(0)
+    back_0 = backward(0)
+    mine = pl.ds(pl.multiple_of(me * SHARE, SHARE), SHARE)
+    total = part[mine, :].astype(f32)
+    for o in range(1, MDL):
+        first[o - 1].wait_recv()
+        total = total + rs1[o].astype(f32)
+    readout[mine, :] = total.astype(bf16)
+    spread = [
+        remote(readout.at[mine], readout.at[mine], ag1_s.at[o], ag1_r.at[o], {"mdl": peers[o]})
+        for o in range(1, MDL)
+    ]
+    prepare(1)
+    back_1 = backward(1)
+    gather_0 = collect(0, back_0)
+    for copy in spread:
+        copy.wait_recv()
+    forward(0)
+    gather_1 = collect(1, back_1)
+    forward(1)
+    for copy in gather_0 + gather_1:
+        copy.wait_recv()
+    gfull[...] = lax.dot_general(rb[...], x_ref[...], tt, preferred_element_type=f32)
+    owner = 1 - core
+    swap = remote(
+        gfull.at[pl.ds(pl.multiple_of(owner * 64, 64), 64)], grecv, dp_s, dp_r, {"dp": owner}
+    )
+    swap.wait_recv()
+    grad_ref[...] = gfull[pl.ds(pl.multiple_of(core * 64, 64), 64), :] + grecv[...]
+    swap.wait_send()
+    for copy in first + spread + back_0 + back_1 + gather_0 + gather_1:
+        copy.wait_send()
+
+
+def fused(layer_input, read_weight, head_inputs, write_vectors, log_decay, segment_ids, out_grad):
+    f32, bf16 = jnp.float32, jnp.bfloat16
+    dma = pltpu.SemaphoreType.DMA
+    vmem = pl.BlockSpec(memory_space=pltpu.VMEM)
+    length = layer_input.shape[1]
+    cols = layer_input.shape[2]
+    state = write_vectors.shape[2]
+    square = (BLOCK_LEN, BLOCK_LEN)
+    return pl.pallas_call(
+        fused_kernel,
+        out_shape=(
+            jax.ShapeDtypeStruct(head_inputs.shape, bf16),
+            jax.ShapeDtypeStruct((state // 2, cols), f32),
+        ),
+        in_specs=[vmem] * 7,
+        out_specs=(vmem, vmem),
+        scratch_shapes=[
+            pltpu.VMEM((length, state), bf16),
+            pltpu.VMEM((MDL, SHARE, state), bf16),
+            pltpu.VMEM((length, state), bf16),
+            pltpu.VMEM((length, state), bf16),
+            pltpu.VMEM((2, MDL, HALF, state), bf16),
+            pltpu.VMEM((length, state), bf16),
+            pltpu.VMEM((state, cols), f32),
+            pltpu.VMEM((state // 2, cols), f32),
+            pltpu.VMEM((48, BLOCK_LEN), f32),
+            pltpu.VMEM((128, BLOCK_LEN), f32),
+            pltpu.VMEM((2, HEAD_N, 1, BLOCK_LEN), f32),
+            pltpu.VMEM((2, HEAD_N, BLOCK_LEN, 128), f32),
+            pltpu.VMEM((PAIRS, BLOCK_LEN, 128), f32),
+            pltpu.VMEM((PAIRS, BLOCK_LEN, 128), f32),
+            pltpu.VMEM((2,) + square, f32),
+            pltpu.VMEM(square, f32),
+            pltpu.VMEM(square, f32),
+            pltpu.VMEM((PAIRS, 128, state), bf16),
+            pltpu.VMEM((BLOCK_LEN, state), f32),
+            dma((MDL,)), dma((MDL,)), dma((MDL,)), dma((MDL,)),
+            dma((2, MDL)), dma((2, MDL)), dma((2, MDL)), dma((2, MDL)),
+            dma, dma,
+        ],
+        compiler_params=pltpu.CompilerParams(
+            collective_id=0, has_side_effects=True, vmem_limit_bytes=56 * 1024 * 1024
+        ),
+    )(
+        layer_input.reshape(length, cols), read_weight, head_inputs, write_vectors,
+        log_decay, segment_ids, out_grad,
+    )
+
+
+def fits(mesh, values):
+    (layer_input, _, head_inputs, write_vectors, log_decay, _, _) = values
+    return (
+        mesh.shape["ctx"] == 1
+        and mesh.shape["mdl"] == MDL
+        and mesh.shape["dp"] == 2
+        and layer_input.shape[:2] == (1, 2 * BLOCK_LEN)
+        and log_decay.shape[1] == HEAD_N
+        and head_inputs.shape[2] == HEAD_N * 64
+        and write_vectors.shape[2] == 128
+    )
+
+
 def solution(mesh):
+    def chosen(*values):
+        if fits(mesh, values):
+            return fused(*values)
+        return per_device(*values)
+
     placed = (
         P(("grp", "dp"), "ctx", "mdl"),
         P("mdl", None),
@@ -163,7 +441,7 @@
         P(("grp", "dp"), "ctx", "mdl"),
     )
     return jax.shard_map(
-        per_device,
+        chosen,
         mesh=mesh,
         in_specs=placed,
         out_specs=(P(("grp", "dp"), "ctx", "mdl"), P(("grp", "ctx", "dp"), "mdl")),

time: 199 us -> 45.1 us (0.23)
  waiting for transfers between devices: 108 us -> 0 us
  Pallas kernels: 0 us -> 37.4 us
  matrix products: 33.6 us -> 0 us
  local copies, waits for them, and re-layouts: 25.3 us -> 6.82 us
  between operations: 14 us -> 0.65 us
  other arithmetic: 12.1 us -> 0 us
  loops' own time: 5.3 us -> 0 us
    psum x2 -> x0, waiting for transfers between devices: 106 us -> none  [the longest x1 70 us: per_device(): read_back = lax.psum(back_part.astype(jnp.bfloat16), 'mdl')]
    pallas_call x0 -> x1, Pallas kernels: none -> 37.4 us  [fused(): pl.pallas_call(fused_kernel, out_shape=(jax.ShapeDtypeStruct(head_inputs....]
    dot_general x13 -> x0, matrix products: 33.6 us -> none  [the longest x2 11.1 us: inside(): jnp.einsum('hts,shp->thp', blend_factor, value_rows, preferred_element_ty...]
    another operation x6 -> x0, local copies, waits for them, and re-layouts: 7.41 us -> none  [the longest x1 3.55 us: per_device(): grads_block.reshape(flat_count, BLOCK_LEN, head_count, head_dim)]
    convert_element_type x7 -> x0, other arithmetic: 5.94 us -> none  [the longest x1 2.27 us: per_device(): (values * jnp.transpose(end_weight, (0, 2, 3, 1))[..., None]).astype(jnp....]
    another operation x2 -> x0, loops' own time: 5.3 us -> none  [the longest x1 5.19 us: per_device(): lax.scan(absorb, neutral, (front_seg, back_seg, through, block_states))]
    unnamed x19 -> x6, local copies, waits for them, and re-layouts: 10.5 us -> 6.82 us
    convert_element_type x4 -> x0, local copies, waits for them, and re-layouts: 3.46 us -> none  [the longest x1 1.81 us: per_device(): read_back = lax.psum(back_part.astype(jnp.bfloat16), 'mdl')]
  transfers between devices with their start and end apart: 3 -> 0, of which waited for: 3 -> 0; matrix products, arithmetic and copies ran while one was open for 19% -> 0% of each run, Pallas kernels for 0% -> 0%
where the time goes in v1:
time: 45.1 us; the launch traced here: 44.8 us
  Pallas kernels  37.4 us (83%)
  local copies, waits for them, and re-layouts  6.82 us (15%)
  between operations  0.65 us (1%)
    pallas_call x1, Pallas kernels, fused(): pl.pallas_call(fused_kernel, out_shape=(jax.ShapeDtypeStruct(head_inputs....  37.4 us
    unnamed x6, local copies, waits for them, and re-layouts  6.82 us

profile of v1, /device:TPU:0, one launch (start us, length us, event | category | flops | bytes accessed | tf_op | source)
XLA Modules:
  0.0 44.8 jit_solution(1126647311906367592)
XLA Ops:
  0.6 1.4 %copy.10.ld_ref = f32[1,10,1024]{2,1,0:T(8,128)} copy(f32[1,10,1024]{2,0,1:T(1,128)} %param.11) | data formatting | bytes 81920 | tf_op args[4]
  2.0 2.2 %copy.9 = bf16[1,1024,320]{2,1,0:T(8,128)(2,1)} copy(bf16[1,1024,320]{1,2,0:T(8,128)(2,1)} %param.7) | data formatting | bytes 1310720 | tf_op args[0]
  4.3 37.4 %shard_map.86 = (bf16[1,1024,640]{2,1,0:T(8,128)(2,1)}, f32[64,320]{1,0:T(8,128)}) custom-call(bf16[1024,320]{1,0:T(8,128)(2,1)} %bitcast.1, bf16[320,128]{1,0:T(8,128)(2,1)} %w_ref.1, bf16[1,1024,640]{2,1,0:T(8,128)(2,1)} %hi_ref.1, bf16[1,1024,128]{2,1,0:T(8,128)(2,1)} %wv_ref.1, f32[1,10,1024]{2,1,0:T(8,128)} %copy.10.ld_ref, s32[1,1024]{1,0:T(1,128)} %seg_ref.1, ...), custom_call_target="tpu_custom_call" | custom-call | tf_op jit(solution)/shard_map/pallas_call | solution.py:374
  41.7 0.0 copy-start
  41.7 2.5 %copy.13 = bf16[1,1024,640]{2,1,0:T(8,128)(2,1)} copy(bf16[1,1024,640]{2,1,0:T(8,128)(2,1)} %get-tuple-element.4) | data formatting | bytes 2621440
  44.2 0.0 copy-done
  44.2 0.6 %copy.14 = f32[64,320]{1,0:T(8,128)} copy(f32[64,320]{1,0:T(8,128)S(1)} %copy-done) | data formatting | bytes 163840
Async XLA Ops:
  41.7 2.5 %copy-start = (f32[64,320]{1,0:T(8,128)S(1)}, f32[64,320]{1,0:T(8,128)}, u32[]{:S(2)}) copy-start(f32[64,320]{1,0:T(8,128)} %get-tuple-element.5) | copy-start | bytes 245764

commit v2 on v1

--- a/solution.py
+++ b/solution.py
@@ -164,12 +164,17 @@
 
 
 def fused_kernel(
-    x_ref, w_ref, hi_ref, wv_ref, ld_ref, seg_ref, og_ref, out_ref, grad_ref,
+    x_ref, w_ref, hi_hbm, wv_ref, ld_ref, seg_ref, og_hbm, out_hbm, grad_ref,
+    hi_ref, og_ref, out_ref, kept,
     part, rs1, readout, back, rs2, rb, gfull, grecv,
     split, stack, rowx, colx, endx, entx, bias, resp, scores, start, carry,
-    rs1_s, rs1_r, ag1_s, ag1_r, rs2_s, rs2_r, ag2_s, ag2_r, dp_s, dp_r,
+    rs1_s, rs1_r, ag1_s, ag1_r, rs2_s, rs2_r, ag2_s, ag2_r, dp_s, dp_r, in_s, out_s,
 ):
     f32, bf16 = jnp.float32, jnp.bfloat16
+    load_hi = pltpu.make_async_copy(hi_hbm, hi_ref, in_s.at[0])
+    load_og = pltpu.make_async_copy(og_hbm, og_ref, in_s.at[1])
+    load_hi.start()
+    load_og.start()
     me = lax.axis_index("mdl")
     core = lax.axis_index("dp")
     peers = [lax.rem(me + o, MDL) for o in range(MDL)]
@@ -186,7 +191,9 @@
         copy.start()
         return copy
 
-    part[...] = jnp.dot(x_ref[...], w_ref[...], preferred_element_type=f32).astype(bf16)
+    nn = (((1,), (1,)), ((), ()))
+    tt = (((0,), (0,)), ((), ()))
+    part[...] = lax.dot_general(x_ref[...], w_ref[...], tt, preferred_element_type=f32).astype(bf16)
     pl.semaphore_wait(barrier, MDL)
     first = [
         remote(
@@ -203,17 +210,17 @@
     rows_i = lax.broadcasted_iota(jnp.int32, (BLOCK_LEN, BLOCK_LEN), 0)
     cols_i = lax.broadcasted_iota(jnp.int32, (BLOCK_LEN, BLOCK_LEN), 1)
     upper = (rows_i <= cols_i).astype(f32).astype(bf16)
-    nn = (((1,), (1,)), ((), ()))
-    tt = (((0,), (0,)), ((), ()))
 
     def prepare(k):
         span = pl.ds(k * BLOCK_LEN, BLOCK_LEN)
         split[...] = jnp.zeros_like(split)
         stack[...] = jnp.zeros_like(stack)
-        rest = ld_ref[0, :, span]
+        for h in range(HEAD_N):
+            stack[pl.ds(h, 1), :] = ld_ref[h, :, span]
+        rest = stack[pl.ds(0, 16), :]
         for piece in range(3):
             high = rest.astype(bf16).astype(f32)
-            split[pl.ds(16 * piece, HEAD_N), :] = high
+            split[pl.ds(16 * piece, 16), :] = high
             rest = rest - high
         sums = jnp.dot(split[...].astype(bf16), upper, preferred_element_type=f32)
         cum = (sums[0:16] + sums[16:32] + sums[32:48]) * LOG2E
@@ -270,9 +277,12 @@
                 grads = og_ref[0, pl.ds(k * BLOCK_LEN + i * TILE, TILE), lanes]
                 pa = lax.dot_general(grads * mask_a, value, nn, preferred_element_type=f32)
                 pb = lax.dot_general(grads * mask_b, value, nn, preferred_element_type=f32)
-                resp[pl.ds(i * TILE, TILE), pl.ds(0, wide)] += (
-                    weight(k, 2 * j, i, wide) * pa + weight(k, 2 * j + 1, i, wide) * pb
-                )
+                wa = weight(k, 2 * j, i, wide)
+                wb = weight(k, 2 * j + 1, i, wide)
+                rows = pl.ds(i * TILE, TILE)
+                kept[k, 2 * j, rows, pl.ds(0, wide)] = wa.astype(bf16)
+                kept[k, 2 * j + 1, rows, pl.ds(0, wide)] = wb.astype(bf16)
+                resp[rows, pl.ds(0, wide)] += wa * pa + wb * pb
             return 0
 
         lax.fori_loop(0, PAIRS, body, 0)
@@ -289,22 +299,19 @@
     def forward(k):
         keys = wv_ref[0, pl.ds(k * BLOCK_LEN, BLOCK_LEN), :]
         reads = readout[pl.ds(k * BLOCK_LEN, BLOCK_LEN), :]
-        scores[...] = lax.dot_general(reads, keys, nn, preferred_element_type=f32)
+        scores[...] = lax.dot_general(reads, keys, nn, preferred_element_type=f32).astype(bf16)
 
         def body(j, _):
             lanes = lanes_of(j)
             for i in range(BLOCK_LEN // TILE):
                 wide = (i + 1) * TILE
                 value = hi_ref[0, pl.ds(k * BLOCK_LEN, wide), lanes]
-                score = scores[pl.ds(i * TILE, TILE), pl.ds(0, wide)]
-                oa = jnp.dot(
-                    (weight(k, 2 * j, i, wide) * score).astype(bf16), value,
-                    preferred_element_type=f32,
-                )
-                ob = jnp.dot(
-                    (weight(k, 2 * j + 1, i, wide) * score).astype(bf16), value,
-                    preferred_element_type=f32,
-                )
+                rows = pl.ds(i * TILE, TILE)
+                score = scores[rows, pl.ds(0, wide)]
+                mix_a = kept[k, 2 * j, rows, pl.ds(0, wide)] * score
+                mix_b = kept[k, 2 * j + 1, rows, pl.ds(0, wide)] * score
+                oa = jnp.dot(mix_a, value, preferred_element_type=f32)
+                ob = jnp.dot(mix_b, value, preferred_element_type=f32)
                 total = jnp.where(left, oa, ob)
                 if k == 1:
                     carried = lax.dot_general(
@@ -316,6 +323,10 @@
             return 0
 
         lax.fori_loop(0, PAIRS, body, 0)
+        span = pl.ds(k * BLOCK_LEN, BLOCK_LEN)
+        store = pltpu.make_async_copy(out_ref.at[:, span], out_hbm.at[:, span], out_s.at[k])
+        store.start()
+        return store
 
     def collect(k, copies):
         mine = pl.ds(pl.multiple_of(k * BLOCK_LEN + me * HALF, HALF), HALF)
@@ -330,6 +341,8 @@
         ]
 
     prepare(0)
+    load_hi.wait()
+    load_og.wait()
     back_0 = backward(0)
     mine = pl.ds(pl.multiple_of(me * SHARE, SHARE), SHARE)
     total = part[mine, :].astype(f32)
@@ -346,12 +359,12 @@
     gather_0 = collect(0, back_0)
     for copy in spread:
         copy.wait_recv()
-    forward(0)
+    store_0 = forward(0)
     gather_1 = collect(1, back_1)
-    forward(1)
+    store_1 = forward(1)
     for copy in gather_0 + gather_1:
         copy.wait_recv()
-    gfull[...] = lax.dot_general(rb[...], x_ref[...], tt, preferred_element_type=f32)
+    gfull[...] = lax.dot_general(rb[...], x_ref[...], (((0,), (1,)), ((), ())), preferred_element_type=f32)
     owner = 1 - core
     swap = remote(
         gfull.at[pl.ds(pl.multiple_of(owner * 64, 64), 64)], grecv, dp_s, dp_r, {"dp": owner}
@@ -359,6 +372,8 @@
     swap.wait_recv()
     grad_ref[...] = gfull[pl.ds(pl.multiple_of(core * 64, 64), 64), :] + grecv[...]
     swap.wait_send()
+    store_0.wait()
+    store_1.wait()
     for copy in first + spread + back_0 + back_1 + gather_0 + gather_1:
         copy.wait_send()
 
@@ -367,6 +382,7 @@
     f32, bf16 = jnp.float32, jnp.bfloat16
     dma = pltpu.SemaphoreType.DMA
     vmem = pl.BlockSpec(memory_space=pltpu.VMEM)
+    anywhere = pl.BlockSpec(memory_space=pl.ANY)
     length = layer_input.shape[1]
     cols = layer_input.shape[2]
     state = write_vectors.shape[2]
@@ -377,9 +393,13 @@
             jax.ShapeDtypeStruct(head_inputs.shape, bf16),
             jax.ShapeDtypeStruct((state // 2, cols), f32),
         ),
-        in_specs=[vmem] * 7,
-        out_specs=(vmem, vmem),
+        in_specs=[vmem, vmem, anywhere, vmem, vmem, vmem, anywhere],
+        out_specs=(anywhere, vmem),
         scratch_shapes=[
+            pltpu.VMEM(head_inputs.shape, bf16),
+            pltpu.VMEM(head_inputs.shape, bf16),
+            pltpu.VMEM(head_inputs.shape, bf16),
+            pltpu.VMEM((2, HEAD_N) + square, bf16),
             pltpu.VMEM((length, state), bf16),
             pltpu.VMEM((MDL, SHARE, state), bf16),
             pltpu.VMEM((length, state), bf16),
@@ -396,19 +416,19 @@
             pltpu.VMEM((PAIRS, BLOCK_LEN, 128), f32),
             pltpu.VMEM((2,) + square, f32),
             pltpu.VMEM(square, f32),
-            pltpu.VMEM(square, f32),
+            pltpu.VMEM(square, bf16),
             pltpu.VMEM((PAIRS, 128, state), bf16),
             pltpu.VMEM((BLOCK_LEN, state), f32),
             dma((MDL,)), dma((MDL,)), dma((MDL,)), dma((MDL,)),
             dma((2, MDL)), dma((2, MDL)), dma((2, MDL)), dma((2, MDL)),
-            dma, dma,
+            dma, dma, dma((2,)), dma((2,)),
         ],
         compiler_params=pltpu.CompilerParams(
             collective_id=0, has_side_effects=True, vmem_limit_bytes=56 * 1024 * 1024
         ),
     )(
-        layer_input.reshape(length, cols), read_weight, head_inputs, write_vectors,
-        log_decay, segment_ids, out_grad,
+        layer_input.reshape(length, cols).T, read_weight, head_inputs, write_vectors,
+        jnp.transpose(log_decay, (1, 0, 2)), segment_ids, out_grad,
     )
 
 

time: 45.1 us -> 39.8 us (0.88)
  local copies, waits for them, and re-layouts: 6.82 us -> 3.16 us
  Pallas kernels: 37.4 us -> 35.9 us
    unnamed x6 -> x4, local copies, waits for them, and re-layouts: 6.82 us -> 3.16 us
    pallas_call x1, Pallas kernels: 37.4 us -> 35.9 us  [fused(): pl.pallas_call(fused_kernel, out_shape=(jax.ShapeDtypeStruct(head_inputs....]
where the time goes in v2:
time: 39.8 us; the launch traced here: 39.7 us
  Pallas kernels  35.9 us (90%)
  local copies, waits for them, and re-layouts  3.16 us (8%)
  between operations  0.65 us (2%)
    pallas_call x1, Pallas kernels, fused(): pl.pallas_call(fused_kernel, out_shape=(jax.ShapeDtypeStruct(head_inputs....  35.9 us
    unnamed x4, local copies, waits for them, and re-layouts  3.16 us

profile of v2, /device:TPU:0, one launch (start us, length us, event | category | flops | bytes accessed | tf_op | source)
XLA Modules:
  0.0 39.7 jit_solution(15775485188721818830)
XLA Ops:
  0.6 35.9 %shard_map.86 = (bf16[1,1024,640]{2,1,0:T(8,128)(2,1)}, f32[64,320]{1,0:T(8,128)}) custom-call(bf16[320,1024]{1,0:T(8,128)(2,1)} %bitcast.4, bf16[320,128]{1,0:T(8,128)(2,1)} %w_ref.1, bf16[1,1024,640]{2,1,0:T(8,128)(2,1)} %hi_hbm.1, bf16[1,1024,128]{2,1,0:T(8,128)(2,1)} %wv_ref.1, f32[10,1,1024]{2,1,0:T(1,128)} %bitcast.5, s32[1,1024]{1,0:T(1,128)} %seg_ref.1, ...), custom_call_target="tpu_custom_call" | custom-call | tf_op jit(solution)/shard_map/pallas_call | solution.py:390
  36.5 0.0 copy-start
  36.5 2.5 %copy.11 = bf16[1,1024,640]{2,1,0:T(8,128)(2,1)} copy(bf16[1,1024,640]{2,1,0:T(8,128)(2,1)} %get-tuple-element.4) | data formatting | bytes 2621440
  39.0 0.0 copy-done
  39.0 0.6 %copy.12 = f32[64,320]{1,0:T(8,128)} copy(f32[64,320]{1,0:T(8,128)S(1)} %copy-done) | data formatting | bytes 163840
Async XLA Ops:
  36.5 2.5 %copy-start = (f32[64,320]{1,0:T(8,128)S(1)}, f32[64,320]{1,0:T(8,128)}, u32[]{:S(2)}) copy-start(f32[64,320]{1,0:T(8,128)} %get-tuple-element.5) | copy-start | bytes 245764

commit v3 on v2

--- a/solution.py
+++ b/solution.py
@@ -328,6 +328,35 @@
         store.start()
         return store
 
+    across = me + 1 - 2 * lax.rem(me, 2)
+    lines = [lax.rem(me + 2 * q, MDL) for q in range(4)]
+    origins = [lax.rem(me + MDL - 2 * q, MDL) for q in range(4)]
+
+    def gather(ref, begin, size, send, recv):
+        mine = pl.ds(pl.multiple_of(begin + me * size, size), size)
+        near = [
+            remote(ref.at[mine], ref.at[mine], send(q), recv(q), {"mdl": lines[q]})
+            for q in (2, 3, 1)
+        ]
+        return near, [remote(ref.at[mine], ref.at[mine], send(4), recv(4), {"mdl": across})]
+
+    def relay(copies, ref, begin, size, send, recv):
+        near, far = copies
+        for at in (2, 1, 0):
+            q = (2, 3, 1)[at]
+            near[at].wait_recv()
+            rows = pl.ds(pl.multiple_of(begin + origins[q] * size, size), size)
+            far.append(
+                remote(ref.at[rows], ref.at[rows], send(4 + q), recv(4 + q), {"mdl": across})
+            )
+        return near + far, far
+
+    sems_1 = (lambda o: ag1_s.at[o]), (lambda o: ag1_r.at[o])
+    sems_2 = [
+        ((lambda o: ag2_s.at[0, o]), (lambda o: ag2_r.at[0, o])),
+        ((lambda o: ag2_s.at[1, o]), (lambda o: ag2_r.at[1, o])),
+    ]
+
     def collect(k, copies):
         mine = pl.ds(pl.multiple_of(k * BLOCK_LEN + me * HALF, HALF), HALF)
         total = back[mine, :].astype(f32)
@@ -335,10 +364,7 @@
             copies[o - 1].wait_recv()
             total = total + rs2[k, o].astype(f32)
         rb[mine, :] = total.astype(bf16)
-        return [
-            remote(rb.at[mine], rb.at[mine], ag2_s.at[k, o], ag2_r.at[k, o], {"mdl": peers[o]})
-            for o in range(1, MDL)
-        ]
+        return gather(rb, k * BLOCK_LEN, HALF, *sems_2[k])
 
     prepare(0)
     load_hi.wait()
@@ -350,19 +376,19 @@
         first[o - 1].wait_recv()
         total = total + rs1[o].astype(f32)
     readout[mine, :] = total.astype(bf16)
-    spread = [
-        remote(readout.at[mine], readout.at[mine], ag1_s.at[o], ag1_r.at[o], {"mdl": peers[o]})
-        for o in range(1, MDL)
-    ]
+    spread = gather(readout, 0, SHARE, *sems_1)
     prepare(1)
     back_1 = backward(1)
+    spread, landing = relay(spread, readout, 0, SHARE, *sems_1)
     gather_0 = collect(0, back_0)
-    for copy in spread:
+    for copy in landing:
         copy.wait_recv()
     store_0 = forward(0)
     gather_1 = collect(1, back_1)
+    gather_0, landing_0 = relay(gather_0, rb, 0, HALF, *sems_2[0])
     store_1 = forward(1)
-    for copy in gather_0 + gather_1:
+    gather_1, landing_1 = relay(gather_1, rb, BLOCK_LEN, HALF, *sems_2[1])
+    for copy in landing_0 + landing_1:
         copy.wait_recv()
     gfull[...] = lax.dot_general(rb[...], x_ref[...], (((0,), (1,)), ((), ())), preferred_element_type=f32)
     owner = 1 - core

time: 39.8 us -> 39.1 us (0.982)
  Pallas kernels: 35.9 us -> 35.1 us
    pallas_call x1, Pallas kernels: 35.9 us -> 35.1 us  [fused(): pl.pallas_call(fused_kernel, out_shape=(jax.ShapeDtypeStruct(head_inputs....]
where the time goes in v3:
time: 39.1 us; the launch traced here: 38.9 us
  Pallas kernels  35.1 us (90%)
  local copies, waits for them, and re-layouts  3.16 us (8%)
  between operations  0.65 us (2%)
    pallas_call x1, Pallas kernels, fused(): pl.pallas_call(fused_kernel, out_shape=(jax.ShapeDtypeStruct(head_inputs....  35.1 us
    unnamed x4, local copies, waits for them, and re-layouts  3.16 us

profile of v3, /device:TPU:0, one launch (start us, length us, event | category | flops | bytes accessed | tf_op | source)
XLA Modules:
  0.0 38.9 jit_solution(1989528304298263730)
XLA Ops:
  0.6 35.1 %shard_map.86 = (bf16[1,1024,640]{2,1,0:T(8,128)(2,1)}, f32[64,320]{1,0:T(8,128)}) custom-call(bf16[320,1024]{1,0:T(8,128)(2,1)} %bitcast.4, bf16[320,128]{1,0:T(8,128)(2,1)} %w_ref.1, bf16[1,1024,640]{2,1,0:T(8,128)(2,1)} %hi_hbm.1, bf16[1,1024,128]{2,1,0:T(8,128)(2,1)} %wv_ref.1, f32[10,1,1024]{2,1,0:T(1,128)} %bitcast.5, s32[1,1024]{1,0:T(1,128)} %seg_ref.1, ...), custom_call_target="tpu_custom_call" | custom-call | tf_op jit(solution)/shard_map/pallas_call | solution.py:416
  35.8 0.0 copy-start
  35.8 2.5 %copy.11 = bf16[1,1024,640]{2,1,0:T(8,128)(2,1)} copy(bf16[1,1024,640]{2,1,0:T(8,128)(2,1)} %get-tuple-element.4) | data formatting | bytes 2621440
  38.3 0.0 copy-done
  38.3 0.6 %copy.12 = f32[64,320]{1,0:T(8,128)} copy(f32[64,320]{1,0:T(8,128)S(1)} %copy-done) | data formatting | bytes 163840
Async XLA Ops:
  35.8 2.5 %copy-start = (f32[64,320]{1,0:T(8,128)S(1)}, f32[64,320]{1,0:T(8,128)}, u32[]{:S(2)}) copy-start(f32[64,320]{1,0:T(8,128)} %get-tuple-element.5) | copy-start | bytes 245764

commit v4 on v3

--- a/solution.py
+++ b/solution.py
@@ -354,7 +354,6 @@
     sems_1 = (lambda o: ag1_s.at[o]), (lambda o: ag1_r.at[o])
     sems_2 = [
         ((lambda o: ag2_s.at[0, o]), (lambda o: ag2_r.at[0, o])),
-        ((lambda o: ag2_s.at[1, o]), (lambda o: ag2_r.at[1, o])),
     ]
 
     def collect(k, copies):
@@ -364,7 +363,12 @@
             copies[o - 1].wait_recv()
             total = total + rs2[k, o].astype(f32)
         rb[mine, :] = total.astype(bf16)
-        return gather(rb, k * BLOCK_LEN, HALF, *sems_2[k])
+        if k == 0:
+            return gather(rb, 0, HALF, *sems_2[0])
+        return [
+            remote(rb.at[mine], rb.at[mine], ag2_s.at[1, o], ag2_r.at[1, o], {"mdl": peers[o]})
+            for o in range(1, MDL)
+        ]
 
     prepare(0)
     load_hi.wait()
@@ -387,10 +391,18 @@
     gather_1 = collect(1, back_1)
     gather_0, landing_0 = relay(gather_0, rb, 0, HALF, *sems_2[0])
     store_1 = forward(1)
-    gather_1, landing_1 = relay(gather_1, rb, BLOCK_LEN, HALF, *sems_2[1])
-    for copy in landing_0 + landing_1:
+    for copy in landing_0:
         copy.wait_recv()
-    gfull[...] = lax.dot_general(rb[...], x_ref[...], (((0,), (1,)), ((), ())), preferred_element_type=f32)
+    turn = (((0,), (1,)), ((), ()))
+    halves = [pl.ds(0, BLOCK_LEN), pl.ds(BLOCK_LEN, BLOCK_LEN)]
+    gfull[...] = lax.dot_general(
+        rb[halves[0], :], x_ref[:, halves[0]], turn, preferred_element_type=f32
+    )
+    for copy in gather_1:
+        copy.wait_recv()
+    gfull[...] += lax.dot_general(
+        rb[halves[1], :], x_ref[:, halves[1]], turn, preferred_element_type=f32
+    )
     owner = 1 - core
     swap = remote(
         gfull.at[pl.ds(pl.multiple_of(owner * 64, 64), 64)], grecv, dp_s, dp_r, {"dp": owner}

time: 39.1 us -> 36.8 us (0.941)
  Pallas kernels: 35.1 us -> 32.8 us
    pallas_call x1, Pallas kernels: 35.1 us -> 32.8 us  [fused(): pl.pallas_call(fused_kernel, out_shape=(jax.ShapeDtypeStruct(head_inputs....]
where the time goes in v4:
time: 36.8 us; the launch traced here: 36.6 us
  Pallas kernels  32.8 us (89%)
  local copies, waits for them, and re-layouts  3.16 us (9%)
  between operations  0.65 us (2%)
    pallas_call x1, Pallas kernels, fused(): pl.pallas_call(fused_kernel, out_shape=(jax.ShapeDtypeStruct(head_inputs....  32.8 us
    unnamed x4, local copies, waits for them, and re-layouts  3.16 us

profile of v4, /device:TPU:0, one launch (start us, length us, event | category | flops | bytes accessed | tf_op | source)
XLA Modules:
  0.0 36.6 jit_solution(16389616990052656795)
XLA Ops:
  0.6 32.8 %shard_map.86 = (bf16[1,1024,640]{2,1,0:T(8,128)(2,1)}, f32[64,320]{1,0:T(8,128)}) custom-call(bf16[320,1024]{1,0:T(8,128)(2,1)} %bitcast.4, bf16[320,128]{1,0:T(8,128)(2,1)} %w_ref.1, bf16[1,1024,640]{2,1,0:T(8,128)(2,1)} %hi_hbm.1, bf16[1,1024,128]{2,1,0:T(8,128)(2,1)} %wv_ref.1, f32[10,1,1024]{2,1,0:T(1,128)} %bitcast.5, s32[1,1024]{1,0:T(1,128)} %seg_ref.1, ...), custom_call_target="tpu_custom_call" | custom-call | tf_op jit(solution)/shard_map/pallas_call | solution.py:428
  33.5 0.0 copy-start
  33.5 2.5 %copy.11 = bf16[1,1024,640]{2,1,0:T(8,128)(2,1)} copy(bf16[1,1024,640]{2,1,0:T(8,128)(2,1)} %get-tuple-element.4) | data formatting | bytes 2621440
  36.0 0.0 copy-done
  36.0 0.6 %copy.12 = f32[64,320]{1,0:T(8,128)} copy(f32[64,320]{1,0:T(8,128)S(1)} %copy-done) | data formatting | bytes 163840
Async XLA Ops:
  33.5 2.5 %copy-start = (f32[64,320]{1,0:T(8,128)S(1)}, f32[64,320]{1,0:T(8,128)}, u32[]{:S(2)}) copy-start(f32[64,320]{1,0:T(8,128)} %get-tuple-element.5) | copy-start | bytes 245764

commit v5 on v4

--- a/solution.py
+++ b/solution.py
@@ -255,7 +255,7 @@
     def lanes_of(j):
         return pl.ds(pl.multiple_of(j * 128, 128), 128)
 
-    def backward(k):
+    def backward(k, between=None):
         resp[...] = jnp.zeros_like(resp)
         carry[...] = jnp.zeros_like(carry)
         keys = wv_ref[0, pl.ds(k * BLOCK_LEN, BLOCK_LEN), :]
@@ -285,16 +285,23 @@
                 resp[rows, pl.ds(0, wide)] += wa * pa + wb * pb
             return 0
 
-        lax.fori_loop(0, PAIRS, body, 0)
+        issued = None
+        if between is None:
+            lax.fori_loop(0, PAIRS, body, 0)
+        else:
+            lax.fori_loop(0, 3, body, 0)
+            issued = between()
+            lax.fori_loop(3, PAIRS, body, 0)
         total = jnp.dot(resp[...].astype(bf16), keys, preferred_element_type=f32) + carry[...]
         back[pl.ds(k * BLOCK_LEN, BLOCK_LEN), :] = total.astype(bf16)
-        return [
+        sent = [
             remote(
                 back.at[pl.ds(pl.multiple_of(k * BLOCK_LEN + peers[o] * HALF, HALF), HALF)],
                 rs2.at[k, o], rs2_s.at[k, o], rs2_r.at[k, o], {"mdl": peers[o]},
             )
             for o in range(1, MDL)
         ]
+        return sent, issued
 
     def forward(k):
         keys = wv_ref[0, pl.ds(k * BLOCK_LEN, BLOCK_LEN), :]
@@ -373,18 +380,20 @@
     prepare(0)
     load_hi.wait()
     load_og.wait()
-    back_0 = backward(0)
+    back_0, _ = backward(0)
     mine = pl.ds(pl.multiple_of(me * SHARE, SHARE), SHARE)
     total = part[mine, :].astype(f32)
     for o in range(1, MDL):
         first[o - 1].wait_recv()
         total = total + rs1[o].astype(f32)
     readout[mine, :] = total.astype(bf16)
-    spread = gather(readout, 0, SHARE, *sems_1)
+    begun = gather(readout, 0, SHARE, *sems_1)
     prepare(1)
-    back_1 = backward(1)
-    spread, landing = relay(spread, readout, 0, SHARE, *sems_1)
-    gather_0 = collect(0, back_0)
+
+    def between():
+        return relay(begun, readout, 0, SHARE, *sems_1), collect(0, back_0)
+
+    back_1, ((spread, landing), gather_0) = backward(1, between)
     for copy in landing:
         copy.wait_recv()
     store_0 = forward(0)

time: 36.8 us -> 37.1 us (level)
  no operation moved by 1% of the time
where the time goes in v5:
time: 37.1 us; the launch traced here: 36.9 us
  Pallas kernels  33.1 us (89%)
  local copies, waits for them, and re-layouts  3.16 us (9%)
  between operations  0.65 us (2%)
    pallas_call x1, Pallas kernels, fused(): pl.pallas_call(fused_kernel, out_shape=(jax.ShapeDtypeStruct(head_inputs....  33.1 us
    unnamed x4, local copies, waits for them, and re-layouts  3.16 us

profile of v5, /device:TPU:0, one launch (start us, length us, event | category | flops | bytes accessed | tf_op | source)
XLA Modules:
  0.0 36.9 jit_solution(15270507941274969495)
XLA Ops:
  0.6 33.1 %shard_map.86 = (bf16[1,1024,640]{2,1,0:T(8,128)(2,1)}, f32[64,320]{1,0:T(8,128)}) custom-call(bf16[320,1024]{1,0:T(8,128)(2,1)} %bitcast.4, bf16[320,128]{1,0:T(8,128)(2,1)} %w_ref.1, bf16[1,1024,640]{2,1,0:T(8,128)(2,1)} %hi_hbm.1, bf16[1,1024,128]{2,1,0:T(8,128)(2,1)} %wv_ref.1, f32[10,1,1024]{2,1,0:T(1,128)} %bitcast.5, s32[1,1024]{1,0:T(1,128)} %seg_ref.1, ...), custom_call_target="tpu_custom_call" | custom-call | tf_op jit(solution)/shard_map/pallas_call | solution.py:437
  33.7 0.0 copy-start
  33.7 2.5 %copy.11 = bf16[1,1024,640]{2,1,0:T(8,128)(2,1)} copy(bf16[1,1024,640]{2,1,0:T(8,128)(2,1)} %get-tuple-element.4) | data formatting | bytes 2621440
  36.2 0.0 copy-done
  36.2 0.6 %copy.12 = f32[64,320]{1,0:T(8,128)} copy(f32[64,320]{1,0:T(8,128)S(1)} %copy-done) | data formatting | bytes 163840
Async XLA Ops:
  33.7 2.5 %copy-start = (f32[64,320]{1,0:T(8,128)S(1)}, f32[64,320]{1,0:T(8,128)}, u32[]{:S(2)}) copy-start(f32[64,320]{1,0:T(8,128)} %get-tuple-element.5) | copy-start | bytes 245764

commit v6 on v4

--- a/solution.py
+++ b/solution.py
@@ -13,6 +13,7 @@
 HEAD_N = 10
 PAIRS = HEAD_N // 2
 TILE = 256
+FAR_FIRST = (4, 5, 3, 6, 2, 7, 1)
 LOG2E = 1.4426950408889634
 
 
@@ -200,7 +201,7 @@
             part.at[pl.ds(pl.multiple_of(peers[o] * SHARE, SHARE), SHARE)], rs1.at[o],
             rs1_s.at[o], rs1_r.at[o], {"mdl": peers[o]},
         )
-        for o in range(1, MDL)
+        for o in FAR_FIRST
     ]
 
     lane = lax.broadcasted_iota(jnp.int32, (1, 128), 1)
@@ -293,7 +294,7 @@
                 back.at[pl.ds(pl.multiple_of(k * BLOCK_LEN + peers[o] * HALF, HALF), HALF)],
                 rs2.at[k, o], rs2_s.at[k, o], rs2_r.at[k, o], {"mdl": peers[o]},
             )
-            for o in range(1, MDL)
+            for o in FAR_FIRST
         ]
 
     def forward(k):
@@ -360,14 +361,14 @@
         mine = pl.ds(pl.multiple_of(k * BLOCK_LEN + me * HALF, HALF), HALF)
         total = back[mine, :].astype(f32)
         for o in range(1, MDL):
-            copies[o - 1].wait_recv()
+            copies[FAR_FIRST.index(o)].wait_recv()
             total = total + rs2[k, o].astype(f32)
         rb[mine, :] = total.astype(bf16)
         if k == 0:
             return gather(rb, 0, HALF, *sems_2[0])
         return [
             remote(rb.at[mine], rb.at[mine], ag2_s.at[1, o], ag2_r.at[1, o], {"mdl": peers[o]})
-            for o in range(1, MDL)
+            for o in FAR_FIRST
         ]
 
     prepare(0)
@@ -377,7 +378,7 @@
     mine = pl.ds(pl.multiple_of(me * SHARE, SHARE), SHARE)
     total = part[mine, :].astype(f32)
     for o in range(1, MDL):
-        first[o - 1].wait_recv()
+        first[FAR_FIRST.index(o)].wait_recv()
         total = total + rs1[o].astype(f32)
     readout[mine, :] = total.astype(bf16)
     spread = gather(readout, 0, SHARE, *sems_1)

time: 36.8 us -> 37.3 us (1.014)
  Pallas kernels: 32.8 us -> 33.4 us
    pallas_call x1, Pallas kernels: 32.8 us -> 33.4 us  [fused(): pl.pallas_call(fused_kernel, out_shape=(jax.ShapeDtypeStruct(head_inputs....]
where the time goes in v6:
time: 37.3 us; the launch traced here: 37.2 us
  Pallas kernels  33.4 us (90%)
  local copies, waits for them, and re-layouts  3.16 us (8%)
  between operations  0.65 us (2%)
    pallas_call x1, Pallas kernels, fused(): pl.pallas_call(fused_kernel, out_shape=(jax.ShapeDtypeStruct(head_inputs....  33.4 us
    unnamed x4, local copies, waits for them, and re-layouts  3.16 us

profile of v6, /device:TPU:0, one launch (start us, length us, event | category | flops | bytes accessed | tf_op | source)
XLA Modules:
  0.0 37.2 jit_solution(8113410772984633385)
XLA Ops:
  0.6 33.4 %shard_map.86 = (bf16[1,1024,640]{2,1,0:T(8,128)(2,1)}, f32[64,320]{1,0:T(8,128)}) custom-call(bf16[320,1024]{1,0:T(8,128)(2,1)} %bitcast.4, bf16[320,128]{1,0:T(8,128)(2,1)} %w_ref.1, bf16[1,1024,640]{2,1,0:T(8,128)(2,1)} %hi_hbm.1, bf16[1,1024,128]{2,1,0:T(8,128)(2,1)} %wv_ref.1, f32[10,1,1024]{2,1,0:T(1,128)} %bitcast.5, s32[1,1024]{1,0:T(1,128)} %seg_ref.1, ...), custom_call_target="tpu_custom_call" | custom-call | tf_op jit(solution)/shard_map/pallas_call | solution.py:429
  34.0 0.0 copy-start
  34.0 2.5 %copy.11 = bf16[1,1024,640]{2,1,0:T(8,128)(2,1)} copy(bf16[1,1024,640]{2,1,0:T(8,128)(2,1)} %get-tuple-element.4) | data formatting | bytes 2621440
  36.5 0.0 copy-done
  36.5 0.6 %copy.12 = f32[64,320]{1,0:T(8,128)} copy(f32[64,320]{1,0:T(8,128)S(1)} %copy-done) | data formatting | bytes 163840
Async XLA Ops:
  34.0 2.5 %copy-start = (f32[64,320]{1,0:T(8,128)S(1)}, f32[64,320]{1,0:T(8,128)}, u32[]{:S(2)}) copy-start(f32[64,320]{1,0:T(8,128)} %get-tuple-element.5) | copy-start | bytes 245764
